TPU v7x, 256 devices: a whole 4x4x8 slice. The times are simulated.
256 devices in a mesh: dp: 16 (over z, core), tensor: 16 (over y, x).
Axes of the slice: x: 4, y: 4, z: 8, core: 2. Of those that a mesh axis runs over, the one named last changes fastest.
Arguments:
- upstream: bfloat16 [4096, 8192], P(('dp', 'tensor')), may hold values from -24 to 24
- out_weight: bfloat16 [8192, 10240], P(None, 'tensor'), may hold values from -0.0625 to 0.0625
- inner: bfloat16 [4096, 10240], P('dp', 'tensor'), may hold values from -6 to 6
- groups_bc: bfloat16 [4096, 8192], P('dp', 'tensor'), may hold values from -1.5 to 1.5
- dt_raw: float32 [160, 4096], P('tensor', 'dp'), may hold values from -3 to 3
- a_log: float32 [160], P('tensor'), may hold values from 0 to 2.77
- skip: float32 [160], P('tensor'), may hold values from 0.5 to 1.5
- dt_bias: float32 [160], P('tensor'), may hold values from -4.5 to -1
- head_counts: int32 [16], replicated, may hold values from 1 to 10, 128 in all
Outputs:
- inner_grad: bfloat16 [4096, 10240], P('dp', 'tensor')
- groups_grad: bfloat16 [4096, 8192], P('dp', 'tensor')
- dt_grad: float32 [160, 4096], P('tensor', 'dp')
- weight_grad: float32 [8192, 10240], P('dp', 'tensor')
- head_grads: float32 [3, 160], P(None, 'tensor')
Inputs may be any that keep to these rules, and one draw needn't show every extreme that they name: `head_counts`: heads in use in each tensor group; the other slots of its 10 are padding; they sum to 128.
All inputs are finite; a program needn't handle non-finite values.
Results may differ from a plain program's by a relative error of at most 0.0029.
Values may be sent and summed in bfloat16 or wider, within the bound.
A program may use at most 128 MiB of HBM per device.

v0:
```python
import jax
import jax.numpy as jnp
from jax import lax
from jax.sharding import PartitionSpec as P

BLOCK = 128


def scan_heads(inner, groups_bc, dt_raw, a_log, skip, dt_bias, active):
    length = inner.shape[0]
    head_slots = a_log.shape[0]
    head_width = inner.shape[1] // head_slots
    state_size = groups_bc.shape[1] // 2
    blocks = length // BLOCK
    highest_precision = lax.Precision.HIGHEST
    values = inner.astype(jnp.float32).reshape(blocks, BLOCK, head_slots, head_width)
    projected = groups_bc.astype(jnp.float32).reshape(blocks, BLOCK, 2 * state_size)
    entry_vectors_list = projected[:, :, :state_size]
    readout_matrix = projected[:, :, state_size:]
    step_sizes = jax.nn.softplus(dt_raw + dt_bias[:, None]).reshape(head_slots, blocks, BLOCK)
    rates = step_sizes * jnp.exp(a_log)[:, None, None]
    totals = jnp.cumsum(rates, axis=2)
    scaled_inputs = values * jnp.transpose(step_sizes, (1, 2, 0))[:, :, :, None]
    score_matrix = jnp.einsum(
        "adw,ahw->adh", readout_matrix, entry_vectors_list, precision=highest_precision
    )
    causal = jnp.arange(BLOCK)[:, None] >= jnp.arange(BLOCK)[None, :]
    decay_gaps = totals[:, :, :, None] - totals[:, :, None, :]
    weight_matrix = jnp.where(causal, jnp.exp(-jnp.where(causal, decay_gaps, 0.0)), 0.0)
    local_portion = jnp.einsum(
        "ocmi,cmi,ciof->cmof",
        weight_matrix,
        score_matrix,
        scaled_inputs,
        precision=highest_precision,
    )
    to_end = jnp.exp(totals - totals[:, :, -1:])
    block_states = jnp.einsum(
        "hbk,bkn,bkhp->bhnp", to_end, entry_vectors_list, scaled_inputs, precision=highest_precision
    )
    running = jnp.zeros((head_slots, state_size, head_width), jnp.float32)
    entering = []
    for position in range(blocks):
        entering.append(running)
        running = (
            jnp.exp(-totals[:, position, -1])[:, None, None] * running + block_states[position]
        )
    entering = jnp.stack(entering)
    carried_part = jnp.einsum(
        "bqn,hbq,bhnp->bqhp",
        readout_matrix,
        jnp.exp(-totals),
        entering,
        precision=highest_precision,
    )
    result = (local_portion + carried_part + skip[None, None, :, None] * values) * active[
        None, None, :, None
    ]
    return result.reshape(length, head_slots * head_width)


def body(upstream, out_weight, inner, groups_bc, dt_raw, a_log, skip, dt_bias, head_counts):
    tensor_rank = lax.axis_index("tensor")
    ranks = jnp.arange(head_counts.shape[0], dtype=jnp.int32)
    used_heads = jnp.sum(jnp.where(ranks == tensor_rank, head_counts, 0))
    active = (jnp.arange(a_log.shape[0], dtype=jnp.int32) < used_heads).astype(jnp.float32)
    incoming = lax.all_gather(upstream, "tensor", axis=0, tiled=True)
    flat_grad = jnp.dot(incoming, out_weight, preferred_element_type=jnp.float32)

    def forward(values, pairs, steps, alog, direct, bias):
        return scan_heads(values, pairs, steps, alog, direct, bias, active)

    outputs, pullback = jax.vjp(forward, inner, groups_bc, dt_raw, a_log, skip, dt_bias)
    inner_grad, groups_grad, dt_grad, alog_grad, skip_grad, bias_grad = pullback(flat_grad)
    outputs_low = outputs.astype(jnp.bfloat16)
    contract = (((0,), (0,)), ((), ()))
    weight_grad = lax.psum_scatter(
        lax.dot_general(incoming, outputs_low, contract, preferred_element_type=jnp.float32),
        "dp",
        scatter_dimension=0,
        tiled=True,
    )
    head_grads = lax.psum(jnp.stack([alog_grad, skip_grad, bias_grad]), "dp")
    return (inner_grad, groups_grad, dt_grad, weight_grad, head_grads)


def solution(mesh):
    return jax.shard_map(
        body,
        mesh=mesh,
        in_specs=(
            P(("dp", "tensor"), None),
            P(None, "tensor"),
            P("dp", "tensor"),
            P("dp", "tensor"),
            P("tensor", "dp"),
            P("tensor"),
            P("tensor"),
            P("tensor"),
            P(),
        ),
        out_specs=(
            P("dp", "tensor"),
            P("dp", "tensor"),
            P("tensor", "dp"),
            P("dp", "tensor"),
            P(None, "tensor"),
        ),
        check_vma=False,
    )
```

profile of v0, /device:TPU:1, one launch (start us, length us, event | category | flops | bytes accessed | tf_op | source)
XLA Modules:
  0.0 228.0 jit_solution(3764967016715279917)
XLA Ops:
  7.2 0.0 all-gather.2.cloned.1.call-start
  7.2 0.7 all-gather.2.cloned.1.call-update
  7.9 0.0 reduce-scatter.2.cloned.1.call-start
  8.0 0.7 exp.30
  8.7 1.3 fusion.106
  10.0 0.6 compare_convert_fusion
  10.6 0.1 mul.136
  10.7 0.1 mul.137
  10.8 0.8 compare_select_fusion.2
  11.6 0.0 copy-start.5
  11.6 0.0 copy-start.4
  11.6 1.2 copy.44
  12.8 0.3 reshape.85
  13.2 0.1 copy_multiply_fusion.1
  13.3 0.6 reduce_window_sum.24
  13.8 0.6 iota_compare_fusion
  14.5 0.2 slice_reduce_fusion
  14.7 0.8 fusion.91
  15.5 55.3 %all-gather.2.cloned.1.call-done = bf16[256,8192]{1,0:T(8,128)(2,1)} async-done(((bf16[16,8192]{1,0:T(8,128)(2,1)}), bf16[256,8192]{1,0:T(8,128)(2,1)}) %all-gather.2.cloned.1.call-update) | async-done | bytes 4194320 | tf_op jit(solution)/shard_map/all_gather | solution.py:67
  70.8 0.0 copy-done.4
  70.8 8.9 %multiply_reduce_fusion.2 = (f32[640]{0:T(1024)}, f32[256,640]{1,0:T(8,128)S(1)}) fusion(f32[640]{0:T(1024)S(1)} %mul.137, bf16[256,640]{1,0:T(8,128)(2,1)S(1)} %copy-done.4, bf16[256,8192]{1,0:T(8,128)(2,1)} %all-gather.2.cloned.1.call-done, bf16[8192,640]{1,0:T(8,128)(2,1)} %param.10), kind=kOutput, calls=%fused_computation.45 | convolution fusion | flops 2685009408 | bytes 15668224 | tf_op jit(solution)/shard_map/dot_general | solution.py:68
  79.7 0.2 copy.39
  79.9 0.3 reshape.82
  80.3 0.7 convolution_bitcast_fusion.3
  81.0 0.2 multiply_reduce_fusion.3
  81.2 0.1 copy.48
  81.3 0.8 multiply_negate_fusion
  82.1 0.7 fusion.45
  82.8 0.7 fusion.104
  83.5 0.7 convolution_bitcast_fusion.2
  84.2 0.1 slice_add_fusion
  84.3 0.0 copy-start.2
  84.4 0.0 copy-start.6
  84.4 0.0 copy-start.15
  84.4 0.0 copy-start.31
  84.4 1.3 multiply_reduce_fusion.1
  85.8 2.8 %fusion.36 = bf16[2,128,10,64]{1,3,2,0:T(8,128)(2,1)S(1)} fusion(f32[2,10,64,128]{3,2,1,0:T(8,128)S(1)} %get-tuple-element.38, f32[2,128,128]{2,1,0:T(8,128)S(1)} %copy-done.2, f32[10,2,128]{2,0,1:T(8,128)S(1)} %reduce_window_sum.24, pred[128,128]{1,0:T(8,128)(4,1)S(1)} %copy-done.15, f32[2,128,10,64]{1,0,3,2:T(2,128)S(1)} %reshape.85, ...), kind=kOutput, calls=%fused_computation.29 | convolution fusion | flops 254443520 | bytes 1816656 | tf_op jit(solution)/shard_map/jvp(ocmi,cmi,ciof->cmof)/dot_general | solution.py:30
  88.6 0.3 copy.52
  88.9 8.6 %convolution_bitcast_fusion = f32[8192,640]{0,1:T(8,128)} fusion(bf16[256,8192]{1,0:T(8,128)(2,1)S(1)} %copy-done, bf16[80,8,2,128]{3,2,1,0:T(2,128)(2,1)S(1)} %bitcast.176), kind=kOutput, calls=%fused_computation | convolution fusion | flops 2684354560 | bytes 25493504 | tf_op jit(solution)/shard_map/dot_general | solution.py:78
  97.5 0.0 reduce-scatter.2.cloned.1.call-update
  97.5 1.3 reduce_sum.105
  98.9 1.3 reduce_sum.106
  100.2 1.2 negate_bitcast_fusion
  101.5 1.4 copy.49
  102.8 3.2 %multiply_reduce_fusion.4 = (f32[2,128,10]{1,2,0:T(8,128)}, bf16[2,128,10,64]{1,3,2,0:T(8,128)(2,1)S(1)}) fusion(f32[2,128,10,64]{1,0,3,2:T(2,128)S(1)} %reshape.85, f32[2,128,10]{1,2,0:T(8,128)} %copy-done.5, f32[10]{0:T(128)} %copy-done.24, f32[2,128,10,64]{1,0,3,2:T(2,128)S(1)} %reshape.82, f32[10]{0:T(128)} %param.15, f32[2,128,128]{2,1,0:T(8,128)} %fusion.91, ...), kind=kOutput, calls=%fused_computation.47 | convolution fusion | flops 254932480 | bytes 2482256 | tf_op jit(solution)/shard_map/transpose(jvp(ocmi,cmi,ciof->cmof))/dot_general | solution.py:30
  106.0 0.3 copy.43
  106.4 0.9 copy.54
  107.3 2.6 %multiply_reduce_fusion = (f32[2,128,128]{2,1,0:T(8,128)S(1)}, f32[2,128,128,10]{2,1,3,0:T(8,128)S(1)}) fusion(f32[10,2,128]{2,0,1:T(8,128)S(1)} %reduce_window_sum.24, pred[128,128]{1,0:T(8,128)(4,1)S(1)} %copy-done.16, f32[2,128,10,64]{1,0,3,2:T(2,128)S(1)} %reshape.85, f32[2,128,10]{1,2,0:T(8,128)S(1)} %copy-done.7, f32[10]{0:T(128)S(1)} %copy-done.26, ...), kind=kOutput, calls=%fused_computation.17 | convolution fusion | flops 253919232 | bytes 2789416 | tf_op jit(solution)/shard_map/transpose(jvp(ocmi,cmi,ciof->cmof))/dot_general | solution.py:30
  110.0 0.0 copy-start.19
  110.0 0.0 copy-start.27
  110.0 0.0 copy-start.32
  110.0 0.8 fusion.69
  111.0 0.1 add_add_fusion
  111.0 2.5 %reduce_window_sum.25 = f32[10,2,128]{2,0,1:T(8,128)S(1)} reduce-window(f32[10,2,128]{2,0,1:T(8,128)S(1)} %add_add_fusion, f32[]{:T(128)} %constant.22.clone.1), window={size=1x1x128 pad=0_0x0_0x0_127}, to_apply=%region_7.8 | reduce-window | flops 325120 | bytes 20484 | tf_op jit(solution)/shard_map/transpose(jvp(jit(cumsum)))/reduce_window_sum | solution.py:22
  113.6 0.1 bitcast_add_fusion
  113.7 0.8 fusion.112
  114.6 25.5 %psum.7 = f32[3,10]{1,0:T(4,128)} all-reduce(f32[3,10]{1,0:T(4,128)S(1)} %pad_maximum_fusion), channel_id=1, replica_groups=mesh['dp'=16,'tensor'=16] {'dp'}, use_global_device_ids=true, to_apply=%region_13.14 | all-reduce | flops 30 | bytes 240 | tf_op jit(solution)/shard_map/psum | solution.py:83
  140.1 1.3 fusion.39
  141.4 1.2 fusion.42
  142.7 0.3 convolution_add_fusion.1
  142.9 0.3 convolution_add_fusion
  143.3 0.7 add_convert_fusion.1
  144.0 74.4 %reduce-scatter.2.cloned.1.call-done = f32[512,640]{0,1:T(8,128)} async-done(((f32[8192,640]{0,1:T(8,128)}), f32[512,640]{0,1:T(8,128)}) %reduce-scatter.2.cloned.1.call-update) | async-done | bytes 1310736 | tf_op jit(solution)/shard_map/reduce_scatter | solution.py:77
  218.4 2.8 %copy.55 = f32[512,640]{1,0:T(8,128)} copy(f32[512,640]{0,1:T(8,128)} %reduce-scatter.2.cloned.1.call-done) | data formatting | bytes 2621440
  (68 shorter events, 0.2 us)
Async XLA Ops:
  7.2 63.6 %all-gather.2.cloned.1.call-start = ((), (), s32[]{:S(2)}) async-start(), calls=%async_computation.1 | async-start | bytes 4456448 | tf_op jit(solution)/shard_map/all_gather | solution.py:67
  7.9 6.7 %copy-start.1 = (bf16[256,512]{1,0:T(8,128)(2,1)S(1)}, bf16[256,512]{1,0:T(8,128)(2,1)}, u32[]{:S(2)}) copy-start(bf16[256,512]{1,0:T(8,128)(2,1)} %param.12) | copy-start | bytes 786436
  7.9 210.5 %reduce-scatter.2.cloned.1.call-start = ((), (), s32[]{:S(2)}) async-start(), calls=%async_computation.2 | async-start | bytes 22282240 | tf_op jit(solution)/shard_map/reduce_scatter | solution.py:77
  8.7 4.5 %copy-start.28 = (f32[10]{0:T(128)}, f32[10]{0:T(128)S(1)}, u32[]{:S(2)}) copy-start(f32[10]{0:T(128)S(1)} %exp.30) | copy-start | bytes 124
  10.6 69.7 %copy-start.24 = (f32[10]{0:T(128)}, f32[10]{0:T(128)S(1)}, u32[]{:S(2)}) copy-start(f32[10]{0:T(128)S(1)} %compare_convert_fusion) | copy-start | bytes 124
  11.6 71.9 %copy-start.5 = (f32[2,128,10]{1,2,0:T(8,128)}, f32[2,128,10]{1,2,0:T(8,128)S(1)}, u32[]{:S(2)}) copy-start(f32[2,128,10]{1,2,0:T(8,128)S(1)} %copy.42) | copy-start | bytes 30724
  11.6 59.2 %copy-start.4 = (bf16[256,640]{1,0:T(8,128)(2,1)S(1)}, bf16[256,640]{1,0:T(8,128)(2,1)}, u32[]{:S(2)}) copy-start(bf16[256,640]{1,0:T(8,128)(2,1)} %param.11) | copy-start | bytes 983044
  14.6 68.2 %copy-start.22 = (f32[10,2]{0,1:T(2,128)}, f32[10,2]{0,1:T(2,128)S(1)}, u32[]{:S(2)}) copy-start(f32[10,2]{0,1:T(2,128)S(1)} %slice_reduce_fusion) | copy-start | bytes 244
  14.6 65.6 %copy-start.10 = (f32[2,128,10]{1,2,0:T(8,128)}, f32[2,128,10]{1,2,0:T(8,128)S(1)}, u32[]{:S(2)}) copy-start(f32[2,128,10]{1,2,0:T(8,128)S(1)} %fusion.101) | copy-start | bytes 30724
  82.8 1.4 copy-start.13
  83.5 0.7 copy-start.8
  83.5 0.8 copy-start.25
  84.3 1.4 copy-start.2
  84.4 1.4 copy-start.6
  84.4 1.4 copy-start.11
  84.4 1.4 copy-start.15
  84.4 1.3 copy-start.31
  85.7 3.2 %copy-start = (bf16[256,8192]{1,0:T(8,128)(2,1)S(1)}, bf16[256,8192]{1,0:T(8,128)(2,1)}, u32[]{:S(2)}) copy-start(bf16[256,8192]{1,0:T(8,128)(2,1)} %all-gather.2.cloned.1.call-done) | copy-start | bytes 12582916
  106.0 1.3 copy-start.7
  106.0 1.3 copy-start.16
  106.0 1.3 copy-start.26
  107.3 2.7 %copy-start.3 = (f32[2,128,128]{2,1,0:T(8,128)S(1)}, f32[2,128,128]{2,1,0:T(8,128)}, u32[]{:S(2)}) copy-start(f32[2,128,128]{2,1,0:T(8,128)} %fusion.91) | copy-start | bytes 393220
  109.9 1.0 copy-start.14
  109.9 1.0 copy-start.17
  109.9 1.0 copy-start.18
  109.9 1.0 copy-start.20
  110.0 1.0 copy-start.23
  110.0 3.6 %copy-start.21 = (f32[2,128,10]{1,2,0:T(8,128)S(1)}, f32[2,128,10]{1,2,0:T(8,128)}, u32[]{:S(2)}) copy-start(f32[2,128,10]{1,2,0:T(8,128)} %get-tuple-element.26) | copy-start | bytes 30724
  110.0 3.6 %copy-start.29 = (f32[10]{0:T(128)S(1)}, f32[10]{0:T(128)}, u32[]{:S(2)}) copy-start(f32[10]{0:T(128)} %copy-done.28) | copy-start | bytes 124
  110.0 3.7 %copy-start.19 = (f32[10,256]{1,0:T(8,128)S(1)}, f32[10,256]{1,0:T(8,128)}, u32[]{:S(2)}) copy-start(f32[10,256]{1,0:T(8,128)} %param.13) | copy-start | bytes 30724
  110.0 3.7 %copy-start.27 = (f32[10]{0:T(128)S(1)}, f32[10]{0:T(128)}, u32[]{:S(2)}) copy-start(f32[10]{0:T(128)} %param.16) | copy-start | bytes 124
  110.0 4.5 %copy-start.32 = (f32[10]{0:T(128)S(1)}, f32[10]{0:T(128)}, u32[]{:S(2)}) copy-start(f32[10]{0:T(128)} %param.14) | copy-start | bytes 124
  110.0 4.5 %copy-start.30 = (f32[10]{0:T(128)S(1)}, f32[10]{0:T(128)}, u32[]{:S(2)}) copy-start(f32[10]{0:T(128)} %reduce_sum.106) | copy-start | bytes 124
  110.0 30.1 %copy-start.12 = (f32[2,128,10]{1,2,0:T(8,128)S(1)}, f32[2,128,10]{1,2,0:T(8,128)}, u32[]{:S(2)}) copy-start(f32[2,128,10]{1,2,0:T(8,128)} %copy-done.10) | copy-start | bytes 30724
  110.9 30.5 %copy-start.9 = (f32[2,128,10]{1,2,0:T(8,128)S(1)}, f32[2,128,10]{1,2,0:T(8,128)}, u32[]{:S(2)}) copy-start(f32[2,128,10]{1,2,0:T(8,128)} %copy-done.8) | copy-start | bytes 30724
Sparse Core Ops, SparseCore 0:
  10.4 60.3 all-gather.1
  97.7 120.7 reduce-scatter.1
where the time goes:
time: 229 us; the launch traced here: 228 us
  waiting for transfers between devices  130 us (57%)
  matrix products  33.4 us (15%)
  blocking collectives  25.5 us (11%)
  between operations  14.7 us (6%)
  other arithmetic  13.5 us (6%)
  local copies, waits for them, and re-layouts  10.5 us (5%)
    reduce_scatter x1, waiting for transfers between devices, body(): lax.psum_scatter(lax.dot_general(incoming, outputs_low, contract, preferr...  74.4 us
    all_gather x1, waiting for transfers between devices, body(): incoming = lax.all_gather(upstream, 'tensor', axis=0, tiled=True)  55.3 us
    psum x1, blocking collectives, body(): head_grads = lax.psum(jnp.stack([alog_grad, skip_grad, bias_grad]), 'dp')  25.5 us
    dot_general x1, matrix products, body(): jnp.dot(incoming, out_weight, preferred_element_type=jnp.float32)  8.86 us
    dot_general x3, matrix products, scan_heads(): jnp.einsum('ocmi,cmi,ciof->cmof', weight_matrix, score_matrix, scaled_inp...  8.59 us
    dot_general x1, matrix products, body(): lax.dot_general(incoming, outputs_low, contract, preferred_element_type=j...  8.57 us
  transfers between devices with their start and end apart: 2, of which 2 were waited for; matrix products, arithmetic and copies ran while one was open for 12% of the time, Pallas kernels for 0%

commit v1 on v0

v1 whole, which is shorter than its diff:
```python
import functools

import jax
import jax.numpy as jnp
from jax import lax
from jax.experimental import pallas as pl
from jax.experimental.pallas import tpu as pltpu
from jax.sharding import PartitionSpec as P

MESH = pl.DeviceIdType.MESH
HIGHEST = lax.Precision.HIGHEST
F32 = jnp.float32
BF16 = jnp.bfloat16

T = 256
HALF = 128
HEADS = 10
PW = 64
WIDTH = HEADS * PW
NSTATE = 256
D = 8192
NDP = 16
NT = 16
NZ = 8
DROWS = D // NDP
AH = D // 2
NT_DIMS = (((1,), (1,)), ((), ()))

KINDS = {
    "M1+": ("u", 1, (0, 0), None),
    "M1-": ("u", -1, (0, 0), None),
    "M2+": ("u", 1, (-1, 0), 0),
    "M2-": ("u", -1, (1, 0), 1),
    "N1+": ("v", 1, (0, 0), None),
    "N1-": ("v", -1, (0, 0), None),
    "N2+": ("v", 1, (-1, 0), None),
    "N2-": ("v", -1, (-1, 0), None),
    "N3+": ("v", 1, (1, 0), None),
    "N3-": ("v", -1, (1, 0), None),
    "N4+": ("v", 1, (2, 0), 0),
    "N4-": ("v", -1, (2, 0), 0),
    "N5+": ("v", 1, (2, 0), 1),
    "N5-": ("v", -1, (2, 0), 1),
    "F1+": ("v", 1, (0, -1), 0),
    "F1-": ("v", -1, (0, 1), 1),
    "F2+": ("v", 1, (-1, -1), 0),
    "F2-": ("v", -1, (-1, 1), 1),
    "F3+": ("v", 1, (1, -1), 0),
    "F3-": ("v", -1, (1, 1), 1),
    "F4+": ("v", 1, (2, -1), 0),
    "F5-": ("v", -1, (2, 1), 1),
}
NAMES = list(KINDS)
NK = len(NAMES)


def remote(src, dst, send_sem, recv_sem, device):
    return pltpu.make_async_remote_copy(
        src_ref=src, dst_ref=dst, send_sem=send_sem, recv_sem=recv_sem, device_id=device, device_id_type=MESH
    )


def split(value):
    high = value.astype(BF16)
    return high, (value - high.astype(F32)).astype(BF16)


def dot(a, b):
    return jnp.dot(a, b, preferred_element_type=F32)


def dot_nt(a, b, precision=None):
    return lax.dot_general(a, b, NT_DIMS, precision=precision, preferred_element_type=F32)


def kernel(
    alog_ref, skip_ref, bias_ref, counts_ref, dtraw_ref, up_ref, w_ref, inner_ref, groups_ref,
    ig_ref, gg_ref, dtg_ref, wg_ref, hg_ref,
    a_buf, b_buf, bst, outs, w_buf, x_buf, bc_buf, rows, cols, pack, score, score_t, yscan, fgrad, dgt, xd, gy, gx, hbuf,
    a_send, a_recv, b_send, b_recv, s_send, s_recv, z_send, z_recv, c_send, c_recv, h_send, h_recv, local,
):
    i = lax.axis_index("dp")
    j = lax.axis_index("tensor")
    z, core = i // 2, i % 2
    y, x = j // 4, j % 4
    pending = []

    up_copy = pltpu.make_async_copy(up_ref, a_buf.at[j], local.at[0])
    up_copy.start()
    in_copy = pltpu.make_async_copy(inner_ref, x_buf, local.at[1])
    in_copy.start()
    bc_copy = pltpu.make_async_copy(groups_ref, bc_buf, local.at[2])
    bc_copy.start()
    w_copy = pltpu.make_async_copy(w_ref, w_buf, local.at[3])
    w_copy.start()

    barrier = pltpu.get_barrier_semaphore()
    peers = [((i + r) % NDP, j) for r in range(1, NDP)]
    peers += [(i, y * 4 + (x + s) % 4) for s in (1, -1)] + [(i, (y + s) % 4 * 4 + x) for s in (1, -1)]
    for peer in peers:
        pl.semaphore_signal(barrier, inc=1, device_id=peer, device_id_type=MESH)

    def slot_of(p, du, dv):
        if p == 0:
            return (y + dv) % 4 * 4 + (x + du) % 4
        return (y + du) % 4 * 4 + (x + dv) % 4

    def part(which, slot, p, q):
        if which == "a":
            size = AH if q is None else AH // 2
            return a_buf.at[slot, :, pl.ds(p * AH + (q or 0) * (AH // 2), size)]
        size = T if q is None else T // 2
        return b_buf.at[slot, pl.ds(p * T + (q or 0) * (T // 2), size), :]

    sems = {"a": (a_send, a_recv), "b": (b_send, b_recv)}

    def message(which, p, name, incoming):
        axis, way, (du, dv), q = KINDS[name]
        if incoming:
            du, dv = (du - way, dv) if axis == "u" else (du, dv - way)
        region = part(which, slot_of(p, du, dv), p, q)
        device = (i, slot_of(p, way, 0) if axis == "u" else slot_of(p, 0, way))
        send, recv = sems[which]
        k = p * NK + NAMES.index(name)
        return remote(region, region, send.at[k], recv.at[k], device)

    def send(which, *names):
        for name in names:
            for p in range(2):
                copy = message(which, p, name, False)
                copy.start()
                pending.append(copy)

    def wait(which, *names):
        for name in names:
            for p in range(2):
                message(which, p, name, True).wait_recv()

    def stage(which, step):
        if step == 0:
            send(which, "M1+", "M1-", "N1+", "N1-")
        elif step == 1:
            wait(which, "M1+", "M1-")
            send(which, "M2+", "M2-", "N2+", "N2-", "N3+", "N3-")
        elif step == 2:
            wait(which, "M2+", "M2-")
            send(which, "N4+", "N4-", "N5+", "N5-")
            wait(which, "N1+", "N1-")
            send(which, "F1+", "F1-")
        elif step == 3:
            wait(which, "N2+", "N2-", "N3+", "N3-")
            send(which, "F2+", "F2-", "F3+", "F3-")
        elif step == 4:
            wait(which, "N4+", "N4-", "N5+", "N5-")
            send(which, "F4+", "F5-")
        else:
            wait(which, "F1+", "F1-", "F2+", "F2-", "F3+", "F3-", "F4+", "F5-")

    def ring_region(dz, c, q):
        slot = (z + dz) % NZ * 2 + c
        if q is None:
            return outs.at[slot]
        return outs.at[slot, pl.ds(q * HALF, HALF), :]

    def ring(k, way, incoming):
        q = None if k < 3 else (0 if way == 1 else 1)
        dz = -way * k - (way if incoming else 0)
        region = ring_region(dz, core, q)
        n = k * 2 + (way + 1) // 2
        return remote(region, region, z_send.at[n], z_recv.at[n], ((z + way) % NZ * 2 + core, j))

    def cross(k, way, incoming):
        q = None if k < 4 else (0 if way == 1 else 1)
        region = ring_region(-way * k, 1 - core if incoming else core, q)
        n = 0 if k == 0 else k * 2 - 1 + (way + 1) // 2
        return remote(region, region, c_send.at[n], c_recv.at[n], (z * 2 + 1 - core, j))

    def ring_stage(step):
        if step > 0:
            for way in (1, -1):
                ring(step - 1, way, True).wait_recv()
        copies = []
        if step < 4:
            copies += [ring(step, way, False) for way in (1, -1)]
        copies += [cross(step, way, False) for way in ((1, -1) if step > 0 else (1,))]
        for copy in copies:
            copy.start()
            pending.append(copy)

    def cross_waits():
        cross(0, 1, True).wait_recv()
        for k in range(1, 5):
            for way in (1, -1):
                cross(k, way, True).wait_recv()

    def swap(r, incoming):
        there = (i - r) % NDP if incoming else (i + r) % NDP
        src = a_buf.at[j, :, pl.ds(pl.multiple_of((i + r) % NDP * DROWS, DROWS), DROWS)]
        return remote(src, bst.at[there if incoming else i], s_send.at[r], s_recv.at[r], ((i + r) % NDP, j))

    def heads_swap(r, incoming):
        there = (i - r) % NDP if incoming else (i + r) % NDP
        return remote(
            hbuf.at[i], hbuf.at[there if incoming else i], h_send.at[r], h_recv.at[r], ((i + r) % NDP, j)
        )

    up_copy.wait()
    pl.semaphore_wait(barrier, len(peers))
    stage("a", 0)
    for r in range(1, NDP):
        copy = swap(r, False)
        copy.start()
        pending.append(copy)
    own = pltpu.make_async_copy(
        a_buf.at[j, :, pl.ds(pl.multiple_of(i * DROWS, DROWS), DROWS)], bst.at[i], local.at[4]
    )
    own.start()

    row16 = lax.broadcasted_iota(jnp.int32, (16, T), 0)

    def fill(ref):
        out = jnp.zeros((16, T), F32)
        for h in range(HEADS):
            out = jnp.where(row16 == h, ref[h], out)
        return out

    rows[0] = jnp.zeros((16, T), F32)
    rows[0, 0:HEADS, :] = dtraw_ref[...]
    shifted = rows[0] + fill(bias_ref)
    dt = jnp.maximum(shifted, 0.0) + jnp.log1p(jnp.exp(-jnp.abs(shifted)))
    slope = 1.0 / (1.0 + jnp.exp(-shifted))
    decay = jnp.exp(fill(alog_ref))
    first = lax.broadcasted_iota(jnp.int32, (T, T), 0)
    second = lax.broadcasted_iota(jnp.int32, (T, T), 1)
    total = jnp.dot(
        dt * decay, jnp.where(first <= second, 1.0, 0.0), precision=HIGHEST, preferred_element_type=F32
    )
    rows[0] = total
    rows[1] = dt
    rows[2] = slope
    rows[3] = decay
    pack[...] = jnp.zeros((HALF, T), F32)
    pack[0:16, :] = total
    pack[16:32, :] = dt
    cols[...] = jnp.transpose(pack[...])

    in_copy.wait()
    bc_copy.wait()
    score[...] = dot_nt(bc_buf[:, NSTATE:], bc_buf[:, :NSTATE])
    score_t[...] = dot_nt(bc_buf[:, :NSTATE], bc_buf[:, NSTATE:])

    used = counts_ref[j]
    left = lax.broadcasted_iota(jnp.int32, (1, HALF), 1) < PW

    def per_lane(value, pair):
        return jnp.where(left, value(2 * pair), value(2 * pair + 1))

    def active(h):
        return jnp.where(h < used, 1.0, 0.0).astype(F32)

    def causal(rows_n, cols_n, row_start, col_start, lower):
        a = lax.broadcasted_iota(jnp.int32, (rows_n, cols_n), 0) + row_start
        b = lax.broadcasted_iota(jnp.int32, (rows_n, cols_n), 1) + col_start
        return a >= b if lower else a <= b

    def forward_pair(pair):
        lanes = slice(pair * HALF, (pair + 1) * HALF)
        values = x_buf[:, lanes]
        lane_skip = per_lane(lambda h: skip_ref[h], pair)
        lane_active = per_lane(active, pair)
        for block in range(2):
            end = (block + 1) * HALF
            here = slice(block * HALF, end)
            sides = []
            for h in (2 * pair, 2 * pair + 1):
                gap = rows[0, h : h + 1, 0:end] - cols[here, h : h + 1]
                gap = jnp.where(causal(HALF, end, block * HALF, 0, True), gap, -1e30)
                weights = jnp.exp(gap) * (score[here, 0:end] * rows[1, h : h + 1, 0:end])
                high, low = split(weights)
                sides.append(dot(high, values[0:end]) + dot(low, values[0:end]))
            scanned = jnp.where(left, sides[0], sides[1])
            yscan[here, lanes] = scanned
            out = (scanned + lane_skip * values[here].astype(F32)) * lane_active
            outs[i, here, lanes] = out.astype(BF16)

    forward_pair(0)
    forward_pair(1)
    stage("a", 1)
    forward_pair(2)
    forward_pair(3)
    forward_pair(4)
    ring_stage(0)
    stage("a", 2)

    own.wait()
    for r in range(1, NDP):
        swap(r, True).wait_recv()
    b_buf[j] = jnp.transpose(bst[...].reshape(NDP * 16, DROWS))
    stage("a", 3)
    ring_stage(1)
    stage("a", 4)
    stage("b", 0)
    w_copy.wait()
    stage("a", 5)

    depth = 1024

    def first_matmul(step, carry):
        at = pl.multiple_of(step * depth, depth)
        block = a_buf[:, :, pl.ds(at, depth)].reshape(T, depth)
        fgrad[...] += dot(block, w_buf[pl.ds(at, depth), :])
        return carry

    fgrad[...] = jnp.zeros((T, WIDTH), F32)
    lax.fori_loop(0, D // depth // 2, first_matmul, 0)
    stage("b", 1)
    lax.fori_loop(D // depth // 2, D // depth, first_matmul, 0)
    ring_stage(2)

    dgt[...] = jnp.zeros((T, T), F32)

    def backward_pair(pair):
        lanes = slice(pair * HALF, (pair + 1) * HALF)
        values = x_buf[:, lanes]
        lane_skip = per_lane(lambda h: skip_ref[h], pair)
        grad = fgrad[:, lanes] * per_lane(active, pair)
        g_high, g_low = split(grad)
        both = jnp.concatenate([g_high, g_low], axis=1)
        for block in range(2):
            start = block * HALF
            here = slice(start, start + HALF)
            sides = []
            for side, h in enumerate((2 * pair, 2 * pair + 1)):
                gap = cols[here, h : h + 1] - rows[0, h : h + 1, start:]
                gap = jnp.where(causal(HALF, T - start, start, start, False), gap, -1e30)
                scale = jnp.exp(gap) * cols[here, 16 + h : 17 + h]
                high, low = split(scale * score_t[here, start:])
                two = dot(high, both[start:])
                sides.append(two[:, :HALF] + two[:, HALF:] + dot(low, g_high[start:]))
                mine = jnp.where(left if side == 0 else jnp.logical_not(left), values[here], jnp.zeros((), BF16))
                outer = dot_nt(jnp.concatenate([mine, mine], axis=1), both[start:])
                dgt[here, start:] += scale * outer
            scanned = jnp.where(left, sides[0], sides[1])
            g_here = grad[here]
            x_here = values[here].astype(F32)
            ig_ref[here, lanes] = (scanned + lane_skip * g_here).astype(BF16)
            xd[here, lanes] = x_here * scanned
            gy[here, lanes] = g_here * yscan[here, lanes]
            gx[here, lanes] = g_here * x_here

    backward_pair(0)
    backward_pair(1)
    stage("b", 2)
    backward_pair(2)
    ring_stage(3)
    backward_pair(3)
    backward_pair(4)
    stage("b", 3)

    head_of = lax.broadcasted_iota(jnp.int32, (16, WIDTH), 1) // PW
    pick = jnp.where(head_of == lax.broadcasted_iota(jnp.int32, (16, WIDTH), 0), 1.0, 0.0)
    entry_sum = dot_nt(pick, xd[...], HIGHEST)
    exit_sum = dot_nt(pick, gy[...], HIGHEST)
    skip_sum = dot_nt(pick, gx[...], HIGHEST)
    rate_grad = jnp.dot(
        entry_sum - exit_sum,
        jnp.where(first >= second, 1.0, 0.0),
        precision=HIGHEST,
        preferred_element_type=F32,
    )
    dt_now, decay_now = rows[1], rows[3]
    raw_grad = (entry_sum / dt_now + rate_grad * decay_now) * rows[2]
    dtg_ref[...] = raw_grad[0:HEADS, :]
    alog_part = jnp.sum(rate_grad * dt_now * decay_now, axis=1, keepdims=True)
    skip_part = jnp.sum(skip_sum, axis=1, keepdims=True)
    bias_part = jnp.sum(raw_grad, axis=1, keepdims=True)
    lane16 = lax.broadcasted_iota(jnp.int32, (16, HALF), 1)
    hbuf[i] = jnp.where(
        lane16 == 0, alog_part, jnp.where(lane16 == 1, skip_part, jnp.where(lane16 == 2, bias_part, 0.0))
    )
    for r in range(1, NDP):
        copy = heads_swap(r, False)
        copy.start()
        pending.append(copy)

    low_high, low_low = split(dgt[...])
    gg_ref[:, :NSTATE] = (dot(low_high, bc_buf[:, NSTATE:]) + dot(low_low, bc_buf[:, NSTATE:])).astype(BF16)
    up_high, up_low = split(jnp.transpose(dgt[...]))
    gg_ref[:, NSTATE:] = (dot(up_high, bc_buf[:, :NSTATE]) + dot(up_low, bc_buf[:, :NSTATE])).astype(BF16)

    ring_stage(4)
    stage("b", 4)
    cross_waits()

    def second_matmul(dv):
        for p in range(2):
            slots = [slot_of(p, du, dv) for du in range(4)]
            left_side = jnp.concatenate([b_buf[s, p * T : (p + 1) * T, :] for s in slots], axis=1)
            right_side = jnp.concatenate(
                [outs[:, pl.ds(pl.multiple_of(s * 16, 16), 16), :].reshape(T, WIDTH) for s in slots], axis=0
            )
            here = slice(p * T, (p + 1) * T)
            if dv == 0:
                wg_ref[here, :] = dot(left_side, right_side)
            else:
                wg_ref[here, :] += dot(left_side, right_side)

    second_matmul(0)
    second_matmul(1)
    second_matmul(-1)
    for r in range(1, NDP):
        heads_swap(r, True).wait_recv()
    tot = hbuf[0]
    for r in range(1, NDP):
        tot = tot + hbuf[r]
    eye = jnp.where(
        lax.broadcasted_iota(jnp.int32, (8, HALF), 0) == lax.broadcasted_iota(jnp.int32, (8, HALF), 1), 1.0, 0.0
    )
    hg_ref[...] = dot_nt(eye, tot, HIGHEST)[0:3, 0:HEADS]
    stage("b", 5)
    second_matmul(2)
    for copy in pending:
        copy.wait_send()


def body(upstream, out_weight, inner, groups_bc, dt_raw, a_log, skip, dt_bias, head_counts):
    smem = pl.BlockSpec(memory_space=pltpu.SMEM)
    vmem = pl.BlockSpec(memory_space=pltpu.VMEM)
    hbm = pl.BlockSpec(memory_space=pl.ANY)
    dma = lambda n: pltpu.SemaphoreType.DMA((n,))
    return pl.pallas_call(
        kernel,
        out_shape=(
            jax.ShapeDtypeStruct((T, WIDTH), BF16),
            jax.ShapeDtypeStruct((T, 2 * NSTATE), BF16),
            jax.ShapeDtypeStruct((HEADS, T), F32),
            jax.ShapeDtypeStruct((DROWS, WIDTH), F32),
            jax.ShapeDtypeStruct((3, HEADS), F32),
        ),
        in_specs=[smem] * 4 + [vmem] + [hbm] * 4,
        out_specs=(vmem,) * 5,
        scratch_shapes=[
            pltpu.VMEM((NT, 16, D), BF16),
            pltpu.VMEM((NT, DROWS, T), BF16),
            pltpu.VMEM((NDP, 16, DROWS), BF16),
            pltpu.VMEM((NDP, T, WIDTH), BF16),
            pltpu.VMEM((D, WIDTH), BF16),
            pltpu.VMEM((T, WIDTH), BF16),
            pltpu.VMEM((T, 2 * NSTATE), BF16),
            pltpu.VMEM((4, 16, T), F32),
            pltpu.VMEM((T, HALF), F32),
            pltpu.VMEM((HALF, T), F32),
            pltpu.VMEM((T, T), F32),
            pltpu.VMEM((T, T), F32),
            pltpu.VMEM((T, WIDTH), F32),
            pltpu.VMEM((T, WIDTH), F32),
            pltpu.VMEM((T, T), F32),
            pltpu.VMEM((T, WIDTH), F32),
            pltpu.VMEM((T, WIDTH), F32),
            pltpu.VMEM((T, WIDTH), F32),
            pltpu.VMEM((NDP, 16, HALF), F32),
            dma(2 * NK), dma(2 * NK), dma(2 * NK), dma(2 * NK),
            dma(NDP), dma(NDP), dma(8), dma(8), dma(9), dma(9), dma(NDP), dma(NDP), dma(5),
        ],
        compiler_params=pltpu.CompilerParams(
            collective_id=0, has_side_effects=True, vmem_limit_bytes=56 * 1024 * 1024
        ),
    )(a_log, skip, dt_bias, head_counts, dt_raw, upstream, out_weight, inner, groups_bc)


def solution(mesh):
    return jax.shard_map(
        body,
        mesh=mesh,
        in_specs=(
            P(("dp", "tensor"), None),
            P(None, "tensor"),
            P("dp", "tensor"),
            P("dp", "tensor"),
            P("tensor", "dp"),
            P("tensor"),
            P("tensor"),
            P("tensor"),
            P(),
        ),
        out_specs=(
            P("dp", "tensor"),
            P("dp", "tensor"),
            P("tensor", "dp"),
            P("dp", "tensor"),
            P(None, "tensor"),
        ),
        check_vma=False,
    )
```

time: 229 us -> 73.4 us (0.32)
  waiting for transfers between devices: 130 us -> 0 us
  Pallas kernels: 0 us -> 64.7 us
  matrix products: 33.4 us -> 0 us
  blocking collectives: 25.5 us -> 0 us
  between operations: 14.7 us -> 0.65 us
  other arithmetic: 13.5 us -> 0 us
  local copies, waits for them, and re-layouts: 10.5 us -> 7.75 us
    reduce_scatter x1 -> x0, waiting for transfers between devices: 74.4 us -> none  [body(): lax.psum_scatter(lax.dot_general(incoming, outputs_low, contract, preferr...]
    pallas_call x0 -> x1, Pallas kernels: none -> 64.7 us  [body(): pl.pallas_call(kernel, out_shape=(jax.ShapeDtypeStruct((T, WIDTH), BF16),...]
    all_gather x1 -> x0, waiting for transfers between devices: 55.3 us -> none  [body(): incoming = lax.all_gather(upstream, 'tensor', axis=0, tiled=True)]
    dot_general x14 -> x0, matrix products: 33.4 us -> none  [the longest x1 8.86 us: body(): jnp.dot(incoming, out_weight, preferred_element_type=jnp.float32)]
    psum x1 -> x0, blocking collectives: 25.5 us -> none  [body(): head_grads = lax.psum(jnp.stack([alog_grad, skip_grad, bias_grad]), 'dp')]
    reduce_sum x6 -> x0, other arithmetic: 5.19 us -> none  [the longest x1 1.33 us: scan_heads(): skip[None, None, :, None] * values]
    unnamed x73 -> x7, local copies, waits for them, and re-layouts: 3.9 us -> 7.75 us
    another operation x4 -> x0, other arithmetic: 3.09 us -> none  [the longest x2 3.07 us: scan_heads(): totals = jnp.cumsum(rates, axis=2)]
  transfers between devices with their start and end apart: 2 -> 0, of which waited for: 2 -> 0; matrix products, arithmetic and copies ran while one was open for 12% -> 0% of each run, Pallas kernels for 0% -> 0%
where the time goes in v1:
time: 73.4 us; the launch traced here: 73.1 us
  Pallas kernels  64.7 us (88%)
  local copies, waits for them, and re-layouts  7.75 us (11%)
    pallas_call x1, Pallas kernels, body(): pl.pallas_call(kernel, out_shape=(jax.ShapeDtypeStruct((T, WIDTH), BF16),...  64.7 us
    unnamed x7, local copies, waits for them, and re-layouts  7.75 us

profile of v1, /device:TPU:1, one launch (start us, length us, event | category | flops | bytes accessed | tf_op | source)
XLA Modules:
  0.0 73.1 jit_solution(8557142955462276450)
XLA Ops:
  0.6 64.7 %shard_map.128 = (bf16[256,640]{1,0:T(8,128)(2,1)}, bf16[256,512]{1,0:T(8,128)(2,1)}, f32[10,256]{1,0:T(8,128)}, f32[512,640]{1,0:T(8,128)}, f32[3,10]{1,0:T(4,128)}) custom-call(f32[10]{0:T(128)} %alog_ref.1, f32[10]{0:T(128)} %skip_ref.1, f32[10]{0:T(128)} %bias_ref.1, s32[16]{0:T(128)} %counts_ref.1, f32[10,256]{1,0:T(8,128)} %dtraw_ref.1, ...), custom_call_target="tpu_custom_call" | custom-call | tf_op jit(solution)/shard_map/pallas_call | solution.py:431
  65.3 1.7 %copy.19 = bf16[256,640]{1,0:T(8,128)(2,1)} copy(bf16[256,640]{1,0:T(8,128)(2,1)} %get-tuple-element.10) | data formatting | bytes 655360
  67.0 1.7 %copy.20 = bf16[256,512]{1,0:T(8,128)(2,1)} copy(bf16[256,512]{1,0:T(8,128)(2,1)} %get-tuple-element.11) | data formatting | bytes 524288
  68.7 1.3 %copy.21 = f32[10,256]{1,0:T(8,128)} copy(f32[10,256]{1,0:T(8,128)} %get-tuple-element.12) | data formatting | bytes 20480
  70.0 0.0 copy-start
  70.0 2.5 %copy.22 = f32[512,640]{1,0:T(8,128)} copy(f32[512,640]{1,0:T(8,128)} %get-tuple-element.13) | data formatting | bytes 2621440
  72.5 0.0 copy-done
  72.5 0.6 copy.23
Async XLA Ops:
  70.0 2.5 %copy-start = (f32[3,10]{1,0:T(4,128)S(1)}, f32[3,10]{1,0:T(4,128)}, u32[]{:S(2)}) copy-start(f32[3,10]{1,0:T(4,128)} %get-tuple-element.14) | copy-start | bytes 364

commit v2 on v1

--- a/solution.py
+++ b/solution.py
@@ -157,41 +157,43 @@
             wait(which, "F1+", "F1-", "F2+", "F2-", "F3+", "F3-", "F4+", "F5-")
 
     def ring_region(dz, c, q):
-        slot = (z + dz) % NZ * 2 + c
-        if q is None:
-            return outs.at[slot]
-        return outs.at[slot, pl.ds(q * HALF, HALF), :]
-
-    def ring(k, way, incoming):
-        q = None if k < 3 else (0 if way == 1 else 1)
-        dz = -way * k - (way if incoming else 0)
-        region = ring_region(dz, core, q)
-        n = k * 2 + (way + 1) // 2
+        return outs.at[(z + dz) % NZ * 2 + c, pl.ds(q * HALF, HALF), :]
+
+    def ring(k, way, q, incoming):
+        region = ring_region(-way * k - (way if incoming else 0), core, q)
+        n = (k * 2 + q) * 2 + (way + 1) // 2
         return remote(region, region, z_send.at[n], z_recv.at[n], ((z + way) % NZ * 2 + core, j))
 
-    def cross(k, way, incoming):
-        q = None if k < 4 else (0 if way == 1 else 1)
+    def cross(k, way, q, incoming):
         region = ring_region(-way * k, 1 - core if incoming else core, q)
-        n = 0 if k == 0 else k * 2 - 1 + (way + 1) // 2
+        n = (k * 2 + q) * 2 + (way + 1) // 2
         return remote(region, region, c_send.at[n], c_recv.at[n], (z * 2 + 1 - core, j))
 
-    def ring_stage(step):
-        if step > 0:
-            for way in (1, -1):
-                ring(step - 1, way, True).wait_recv()
-        copies = []
-        if step < 4:
-            copies += [ring(step, way, False) for way in (1, -1)]
-        copies += [cross(step, way, False) for way in ((1, -1) if step > 0 else (1,))]
-        for copy in copies:
-            copy.start()
-            pending.append(copy)
+    def goes(k, way, q):
+        return k < 3 or q == (0 if way == 1 else 1)
+
+    def ring_stage(step, q):
+        for way in (1, -1):
+            if step > 0:
+                if not goes(step - 1, way, q):
+                    continue
+                ring(step - 1, way, q, True).wait_recv()
+            copies = []
+            if step < 4 and goes(step, way, q):
+                copies.append(ring(step, way, q, False))
+            if step > 0 or way == 1:
+                copies.append(cross(step, way, q, False))
+            for copy in copies:
+                copy.start()
+                pending.append(copy)
 
     def cross_waits():
-        cross(0, 1, True).wait_recv()
-        for k in range(1, 5):
-            for way in (1, -1):
-                cross(k, way, True).wait_recv()
+        for q in range(2):
+            cross(0, 1, q, True).wait_recv()
+            for k in range(1, 5):
+                for way in (1, -1):
+                    if goes(k - 1, way, q):
+                        cross(k, way, q, True).wait_recv()
 
     def swap(r, incoming):
         there = (i - r) % NDP if incoming else (i + r) % NDP
@@ -289,7 +291,8 @@
     forward_pair(2)
     forward_pair(3)
     forward_pair(4)
-    ring_stage(0)
+    ring_stage(0, 0)
+    ring_stage(0, 1)
     stage("a", 2)
 
     own.wait()
@@ -297,10 +300,12 @@
         swap(r, True).wait_recv()
     b_buf[j] = jnp.transpose(bst[...].reshape(NDP * 16, DROWS))
     stage("a", 3)
-    ring_stage(1)
+    ring_stage(1, 0)
     stage("a", 4)
     stage("b", 0)
+    ring_stage(1, 1)
     w_copy.wait()
+    ring_stage(2, 0)
     stage("a", 5)
 
     depth = 1024
@@ -313,9 +318,9 @@
 
     fgrad[...] = jnp.zeros((T, WIDTH), F32)
     lax.fori_loop(0, D // depth // 2, first_matmul, 0)
+    ring_stage(2, 1)
+    lax.fori_loop(D // depth // 2, D // depth, first_matmul, 0)
     stage("b", 1)
-    lax.fori_loop(D // depth // 2, D // depth, first_matmul, 0)
-    ring_stage(2)
 
     dgt[...] = jnp.zeros((T, T), F32)
 
@@ -350,12 +355,12 @@
 
     backward_pair(0)
     backward_pair(1)
+    ring_stage(3, 0)
+    backward_pair(2)
     stage("b", 2)
-    backward_pair(2)
-    ring_stage(3)
     backward_pair(3)
+    ring_stage(3, 1)
     backward_pair(4)
-    stage("b", 3)
 
     head_of = lax.broadcasted_iota(jnp.int32, (16, WIDTH), 1) // PW
     pick = jnp.where(head_of == lax.broadcasted_iota(jnp.int32, (16, WIDTH), 0), 1.0, 0.0)
@@ -388,7 +393,9 @@
     up_high, up_low = split(jnp.transpose(dgt[...]))
     gg_ref[:, NSTATE:] = (dot(up_high, bc_buf[:, :NSTATE]) + dot(up_low, bc_buf[:, :NSTATE])).astype(BF16)
 
-    ring_stage(4)
+    stage("b", 3)
+    ring_stage(4, 0)
+    ring_stage(4, 1)
     stage("b", 4)
     cross_waits()
 
@@ -423,20 +430,30 @@
         copy.wait_send()
 
 
+def publish(*refs):
+    sems = refs[10]
+    copies = [pltpu.make_async_copy(refs[n], refs[5 + n], sems.at[n]) for n in range(5)]
+    for copy in copies:
+        copy.start()
+    for copy in copies:
+        copy.wait()
+
+
 def body(upstream, out_weight, inner, groups_bc, dt_raw, a_log, skip, dt_bias, head_counts):
     smem = pl.BlockSpec(memory_space=pltpu.SMEM)
     vmem = pl.BlockSpec(memory_space=pltpu.VMEM)
     hbm = pl.BlockSpec(memory_space=pl.ANY)
     dma = lambda n: pltpu.SemaphoreType.DMA((n,))
-    return pl.pallas_call(
+    shapes = (
+        ((T, WIDTH), BF16),
+        ((T, 2 * NSTATE), BF16),
+        ((HEADS, T), F32),
+        ((DROWS, WIDTH), F32),
+        ((3, HEADS), F32),
+    )
+    results = pl.pallas_call(
         kernel,
-        out_shape=(
-            jax.ShapeDtypeStruct((T, WIDTH), BF16),
-            jax.ShapeDtypeStruct((T, 2 * NSTATE), BF16),
-            jax.ShapeDtypeStruct((HEADS, T), F32),
-            jax.ShapeDtypeStruct((DROWS, WIDTH), F32),
-            jax.ShapeDtypeStruct((3, HEADS), F32),
-        ),
+        out_shape=tuple(pltpu.VMEM(*one) for one in shapes),
         in_specs=[smem] * 4 + [vmem] + [hbm] * 4,
         out_specs=(vmem,) * 5,
         scratch_shapes=[
@@ -460,12 +477,19 @@
             pltpu.VMEM((T, WIDTH), F32),
             pltpu.VMEM((NDP, 16, HALF), F32),
             dma(2 * NK), dma(2 * NK), dma(2 * NK), dma(2 * NK),
-            dma(NDP), dma(NDP), dma(8), dma(8), dma(9), dma(9), dma(NDP), dma(NDP), dma(5),
+            dma(NDP), dma(NDP), dma(16), dma(16), dma(20), dma(20), dma(NDP), dma(NDP), dma(5),
         ],
         compiler_params=pltpu.CompilerParams(
             collective_id=0, has_side_effects=True, vmem_limit_bytes=56 * 1024 * 1024
         ),
     )(a_log, skip, dt_bias, head_counts, dt_raw, upstream, out_weight, inner, groups_bc)
+    return pl.pallas_call(
+        publish,
+        out_shape=tuple(jax.ShapeDtypeStruct(*one) for one in shapes),
+        in_specs=[vmem] * 5,
+        out_specs=(hbm,) * 5,
+        scratch_shapes=[dma(5)],
+    )(*[pltpu.with_memory_space_constraint(one, pltpu.VMEM) for one in results])
 
 
 def solution(mesh):

time: 73.4 us -> 62.4 us (0.85)
  local copies, waits for them, and re-layouts: 7.75 us -> 0 us
  Pallas kernels: 64.7 us -> 61.6 us
    unnamed x7 -> x0, local copies, waits for them, and re-layouts: 7.75 us -> none
    pallas_call x1 -> x2, Pallas kernels: 64.7 us -> 61.6 us  [the longest x1 60.3 us: body(): pl.pallas_call(kernel, out_shape=tuple((pltpu.VMEM(*one) for one in shape...]
where the time goes in v2:
time: 62.4 us; the launch traced here: 62.3 us
  Pallas kernels  61.6 us (99%)
  between operations  0.64 us (1%)
    pallas_call x1, Pallas kernels, body(): pl.pallas_call(kernel, out_shape=tuple((pltpu.VMEM(*one) for one in shape...  60.3 us
    pallas_call x1, Pallas kernels, body(): pl.pallas_call(publish, out_shape=tuple((jax.ShapeDtypeStruct(*one) for o...  1.3 us

profile of v2, /device:TPU:1, one launch (start us, length us, event | category | flops | bytes accessed | tf_op | source)
XLA Modules:
  0.0 62.3 jit_solution(2061077510231515813)
XLA Ops:
  0.6 60.3 %shard_map.128 = (bf16[256,640]{1,0:T(8,128)(2,1)S(1)}, bf16[256,512]{1,0:T(8,128)(2,1)S(1)}, f32[10,256]{1,0:T(8,128)S(1)}, f32[512,640]{1,0:T(8,128)S(1)}, f32[3,10]{1,0:T(4,128)S(1)}) custom-call(f32[10]{0:T(128)} %alog_ref.1, f32[10]{0:T(128)} %skip_ref.1, f32[10]{0:T(128)} %bias_ref.1, s32[16]{0:T(128)} %counts_ref.1, f32[10,256]{1,0:T(8,128)} %dtraw_ref.1, ...), custom_call_target="tpu_custom_call" | custom-call | tf_op jit(solution)/shard_map/pallas_call | solution.py:454
  61.0 1.3 %shard_map.129 = (bf16[256,640]{1,0:T(8,128)(2,1)}, bf16[256,512]{1,0:T(8,128)(2,1)}, f32[10,256]{1,0:T(8,128)}, f32[512,640]{1,0:T(8,128)}, f32[3,10]{1,0:T(4,128)}) custom-call(bf16[256,640]{1,0:T(8,128)(2,1)S(1)} %get-tuple-element.10.refs_0_, bf16[256,512]{1,0:T(8,128)(2,1)S(1)} %get-tuple-element.11.refs_1_, f32[10,256]{1,0:T(8,128)S(1)} %get-tuple-element.12.refs_2_, ...), custom_call_target="tpu_custom_call" | custom-call | tf_op jit(solution)/shard_map/pallas_call | solution.py:486

commit v3 on v2

--- a/solution.py
+++ b/solution.py
@@ -25,6 +25,13 @@
 DROWS = D // NDP
 AH = D // 2
 NT_DIMS = (((1,), (1,)), ((), ()))
+TN_DIMS = (((0,), (0,)), ((), ()))
+
+PLACES = [(dz, c) for dz in (2, 3, 5, 6) for c in (0, 1)] + [(1, 1), (7, 1), (4, 0), (4, 1)]
+PLACES += [(0, 0), (0, 1), (1, 0), (7, 0)]
+FAR = 12
+MOST = 10
+KB = FAR * 16
 
 KINDS = {
     "M1+": ("u", 1, (0, 0), None),
@@ -69,15 +76,19 @@
     return jnp.dot(a, b, preferred_element_type=F32)
 
 
+def dot_tn(a, b):
+    return lax.dot_general(a, b, TN_DIMS, preferred_element_type=F32)
+
+
 def dot_nt(a, b, precision=None):
     return lax.dot_general(a, b, NT_DIMS, precision=precision, preferred_element_type=F32)
 
 
 def kernel(
-    alog_ref, skip_ref, bias_ref, counts_ref, dtraw_ref, up_ref, w_ref, inner_ref, groups_ref,
+    alog_hbm, skip_hbm, bias_hbm, counts_hbm, dtraw_hbm, up_ref, w_ref, inner_ref, groups_ref,
     ig_ref, gg_ref, dtg_ref, wg_ref, hg_ref,
-    a_buf, b_buf, bst, outs, w_buf, x_buf, bc_buf, rows, cols, pack, score, score_t, yscan, fgrad, dgt, xd, gy, gx, hbuf,
-    a_send, a_recv, b_send, b_recv, s_send, s_recv, z_send, z_recv, c_send, c_recv, h_send, h_recv, local,
+    alog_ref, skip_ref, bias_ref, counts_ref, dtraw_ref, a_buf, b_buf, near, outs, w_buf, x_buf, bc_buf, rows, cols, pack, score, score_t, yscan, fgrad, dgt, xd, gy, gx, hbuf,
+    a_send, a_recv, b_send, b_recv, s_send, s_recv, n_send, n_recv, z_send, z_recv, c_send, c_recv, h_send, h_recv, local,
 ):
     i = lax.axis_index("dp")
     j = lax.axis_index("tensor")
@@ -85,20 +96,28 @@
     y, x = j // 4, j % 4
     pending = []
 
-    up_copy = pltpu.make_async_copy(up_ref, a_buf.at[j], local.at[0])
-    up_copy.start()
-    in_copy = pltpu.make_async_copy(inner_ref, x_buf, local.at[1])
-    in_copy.start()
-    bc_copy = pltpu.make_async_copy(groups_ref, bc_buf, local.at[2])
-    bc_copy.start()
-    w_copy = pltpu.make_async_copy(w_ref, w_buf, local.at[3])
-    w_copy.start()
-
     barrier = pltpu.get_barrier_semaphore()
-    peers = [((i + r) % NDP, j) for r in range(1, NDP)]
-    peers += [(i, y * 4 + (x + s) % 4) for s in (1, -1)] + [(i, (y + s) % 4 * 4 + x) for s in (1, -1)]
+    peers = [(i, y * 4 + (x + s) % 4) for s in (1, -1)] + [(i, (y + s) % 4 * 4 + x) for s in (1, -1)]
+    peers += [((i + r) % NDP, j) for r in range(1, NDP)]
     for peer in peers:
         pl.semaphore_signal(barrier, inc=1, device_id=peer, device_id_type=MESH)
+
+    def fetch(n, src, dst):
+        copy = pltpu.make_async_copy(src, dst, local.at[n])
+        copy.start()
+        return copy
+
+    up_copy = fetch(0, up_ref, a_buf.at[j])
+    small = [
+        fetch(4, alog_hbm, alog_ref),
+        fetch(5, skip_hbm, skip_ref),
+        fetch(6, bias_hbm, bias_ref),
+        fetch(7, counts_hbm, counts_ref),
+        fetch(8, dtraw_hbm, dtraw_ref),
+    ]
+    bc_copy = fetch(2, groups_ref, bc_buf)
+    in_copy = fetch(1, inner_ref, x_buf)
+    w_copy = fetch(3, w_ref, w_buf)
 
     def slot_of(p, du, dv):
         if p == 0:
@@ -110,7 +129,7 @@
             size = AH if q is None else AH // 2
             return a_buf.at[slot, :, pl.ds(p * AH + (q or 0) * (AH // 2), size)]
         size = T if q is None else T // 2
-        return b_buf.at[slot, pl.ds(p * T + (q or 0) * (T // 2), size), :]
+        return b_buf.at[slot, :, pl.ds(p * T + (q or 0) * (T // 2), size)]
 
     sems = {"a": (a_send, a_recv), "b": (b_send, b_recv)}
 
@@ -156,18 +175,23 @@
         else:
             wait(which, "F1+", "F1-", "F2+", "F2-", "F3+", "F3-", "F4+", "F5-")
 
-    def ring_region(dz, c, q):
-        return outs.at[(z + dz) % NZ * 2 + c, pl.ds(q * HALF, HALF), :]
+    def place(dz, other):
+        return PLACES.index((dz % NZ, other))
+
+    def half_block(at, q):
+        return outs.at[at, pl.ds(q * HALF, HALF), :]
 
     def ring(k, way, q, incoming):
-        region = ring_region(-way * k - (way if incoming else 0), core, q)
+        here, there = half_block(place(-way * k, 0), q), half_block(place(-way * (k + 1), 0), q)
         n = (k * 2 + q) * 2 + (way + 1) // 2
-        return remote(region, region, z_send.at[n], z_recv.at[n], ((z + way) % NZ * 2 + core, j))
+        return remote(
+            there if incoming else here, there, z_send.at[n], z_recv.at[n], ((z + way) % NZ * 2 + core, j)
+        )
 
     def cross(k, way, q, incoming):
-        region = ring_region(-way * k, 1 - core if incoming else core, q)
+        here, there = half_block(place(-way * k, 0), q), half_block(place(-way * k, 1), q)
         n = (k * 2 + q) * 2 + (way + 1) // 2
-        return remote(region, region, c_send.at[n], c_recv.at[n], (z * 2 + 1 - core, j))
+        return remote(there if incoming else here, there, c_send.at[n], c_recv.at[n], (z * 2 + 1 - core, j))
 
     def goes(k, way, q):
         return k < 3 or q == (0 if way == 1 else 1)
@@ -187,18 +211,44 @@
                 copy.start()
                 pending.append(copy)
 
-    def cross_waits():
-        for q in range(2):
-            cross(0, 1, q, True).wait_recv()
-            for k in range(1, 5):
-                for way in (1, -1):
+    def cross_waits(hops):
+        for k in hops:
+            for q in range(2):
+                for way in (1, -1) if k > 0 else (1,):
                     if goes(k - 1, way, q):
                         cross(k, way, q, True).wait_recv()
 
-    def swap(r, incoming):
-        there = (i - r) % NDP if incoming else (i + r) % NDP
-        src = a_buf.at[j, :, pl.ds(pl.multiple_of((i + r) % NDP * DROWS, DROWS), DROWS)]
-        return remote(src, bst.at[there if incoming else i], s_send.at[r], s_recv.at[r], ((i + r) % NDP, j))
+    def columns(dp):
+        return pl.ds(pl.multiple_of(dp * DROWS, DROWS), DROWS)
+
+    def at_place(dz, other):
+        return (z + dz) % NZ * 2 + (core + other) % 2
+
+    def swap(n, incoming):
+        dz, other = PLACES[n]
+        to = at_place(-dz, other)
+        dst = b_buf.at[j, pl.ds(n * 16, 16), :]
+        src = dst if incoming else a_buf.at[j, :, columns(to)]
+        return remote(src, dst, s_send.at[n], s_recv.at[n], (to, j))
+
+    def near_swap(n, half, incoming):
+        dz, other = PLACES[FAR + 1 + n]
+        to = at_place(-dz, other)
+        dst = near.at[n, :, :, pl.ds(half * T, T)]
+        src = a_buf.at[:, :, pl.ds(pl.multiple_of(to * DROWS + half * T, T), T)]
+        k = n * 2 + half
+        return remote(dst if incoming else src, dst, n_send.at[k], n_recv.at[k], (to, j))
+
+    def near_send(half, *which):
+        for n in which:
+            copy = near_swap(n, half, False)
+            copy.start()
+            pending.append(copy)
+
+    def near_wait(*which):
+        for n in which:
+            for half in range(2):
+                near_swap(n, half, True).wait_recv()
 
     def heads_swap(r, incoming):
         there = (i - r) % NDP if incoming else (i + r) % NDP
@@ -209,14 +259,12 @@
     up_copy.wait()
     pl.semaphore_wait(barrier, len(peers))
     stage("a", 0)
-    for r in range(1, NDP):
-        copy = swap(r, False)
+    for n in range(FAR):
+        copy = swap(n, False)
         copy.start()
         pending.append(copy)
-    own = pltpu.make_async_copy(
-        a_buf.at[j, :, pl.ds(pl.multiple_of(i * DROWS, DROWS), DROWS)], bst.at[i], local.at[4]
-    )
-    own.start()
+    for copy in small:
+        copy.wait()
 
     row16 = lax.broadcasted_iota(jnp.int32, (16, T), 0)
 
@@ -283,7 +331,7 @@
             scanned = jnp.where(left, sides[0], sides[1])
             yscan[here, lanes] = scanned
             out = (scanned + lane_skip * values[here].astype(F32)) * lane_active
-            outs[i, here, lanes] = out.astype(BF16)
+            outs[FAR, here, lanes] = out.astype(BF16)
 
     forward_pair(0)
     forward_pair(1)
@@ -294,19 +342,19 @@
     ring_stage(0, 0)
     ring_stage(0, 1)
     stage("a", 2)
-
-    own.wait()
-    for r in range(1, NDP):
-        swap(r, True).wait_recv()
-    b_buf[j] = jnp.transpose(bst[...].reshape(NDP * 16, DROWS))
+    for n in range(FAR):
+        swap(n, True).wait_recv()
+    ring_stage(1, 0)
     stage("a", 3)
-    ring_stage(1, 0)
+    ring_stage(1, 1)
     stage("a", 4)
     stage("b", 0)
-    ring_stage(1, 1)
+    ring_stage(2, 0)
     w_copy.wait()
-    ring_stage(2, 0)
     stage("a", 5)
+    near_send(0, 0)
+    near_send(1, 0)
+    ring_stage(2, 1)
 
     depth = 1024
 
@@ -318,9 +366,10 @@
 
     fgrad[...] = jnp.zeros((T, WIDTH), F32)
     lax.fori_loop(0, D // depth // 2, first_matmul, 0)
-    ring_stage(2, 1)
+    stage("b", 1)
     lax.fori_loop(D // depth // 2, D // depth, first_matmul, 0)
-    stage("b", 1)
+    ring_stage(3, 0)
+    near_send(0, 1, 2)
 
     dgt[...] = jnp.zeros((T, T), F32)
 
@@ -355,9 +404,8 @@
 
     backward_pair(0)
     backward_pair(1)
-    ring_stage(3, 0)
+    stage("b", 2)
     backward_pair(2)
-    stage("b", 2)
     backward_pair(3)
     ring_stage(3, 1)
     backward_pair(4)
@@ -387,34 +435,54 @@
         copy = heads_swap(r, False)
         copy.start()
         pending.append(copy)
-
+    near_send(1, 1, 2)
+
+    stage("b", 3)
     low_high, low_low = split(dgt[...])
     gg_ref[:, :NSTATE] = (dot(low_high, bc_buf[:, NSTATE:]) + dot(low_low, bc_buf[:, NSTATE:])).astype(BF16)
     up_high, up_low = split(jnp.transpose(dgt[...]))
     gg_ref[:, NSTATE:] = (dot(up_high, bc_buf[:, :NSTATE]) + dot(up_low, bc_buf[:, :NSTATE])).astype(BF16)
 
-    stage("b", 3)
+    def second_matmul(dvs, low, high):
+        for p in range(2):
+            slots = [slot_of(p, du, dv) for dv in dvs for du in range(4)]
+            here = slice(p * T, (p + 1) * T)
+            left_side = jnp.concatenate([b_buf[s, low * 16 : high * 16, here] for s in slots], axis=0)
+            right_side = jnp.concatenate(
+                [
+                    outs[low:high, pl.ds(pl.multiple_of(s * 16, 16), 16), :].reshape((high - low) * 16, WIDTH)
+                    for s in slots
+                ],
+                axis=0,
+            )
+            wg_ref[here, :] += dot_tn(left_side, right_side)
+
+    def chip_matmul():
+        for p in range(2):
+            here = slice(p * T, (p + 1) * T)
+            mine = a_buf[:, :, pl.ds(pl.multiple_of(i * DROWS + p * T, T), T)].reshape(T, T)
+            left_side = jnp.concatenate([mine, near[0, :, :, here].reshape(T, T)], axis=0)
+            wg_ref[here, :] = dot_tn(left_side, outs[FAR : FAR + 2, :, :].reshape(2 * T, WIDTH))
+
+    def near_matmul():
+        for p in range(2):
+            here = slice(p * T, (p + 1) * T)
+            left_side = near[1:3, :, :, here].reshape(2 * T, T)
+            wg_ref[here, :] += dot_tn(left_side, outs[FAR + 2 :, :, :].reshape(2 * T, WIDTH))
+
+    near_wait(0)
+    cross_waits((0, 1, 2, 3))
+    chip_matmul()
+    second_matmul((0,), 0, MOST)
+    stage("b", 4)
     ring_stage(4, 0)
     ring_stage(4, 1)
-    stage("b", 4)
-    cross_waits()
-
-    def second_matmul(dv):
-        for p in range(2):
-            slots = [slot_of(p, du, dv) for du in range(4)]
-            left_side = jnp.concatenate([b_buf[s, p * T : (p + 1) * T, :] for s in slots], axis=1)
-            right_side = jnp.concatenate(
-                [outs[:, pl.ds(pl.multiple_of(s * 16, 16), 16), :].reshape(T, WIDTH) for s in slots], axis=0
-            )
-            here = slice(p * T, (p + 1) * T)
-            if dv == 0:
-                wg_ref[here, :] = dot(left_side, right_side)
-            else:
-                wg_ref[here, :] += dot(left_side, right_side)
-
-    second_matmul(0)
-    second_matmul(1)
-    second_matmul(-1)
+    second_matmul((1,), 0, MOST)
+    second_matmul((-1,), 0, MOST)
+    cross_waits((4,))
+    second_matmul((0, 1, -1), MOST, FAR)
+    near_wait(1, 2)
+    near_matmul()
     for r in range(1, NDP):
         heads_swap(r, True).wait_recv()
     tot = hbuf[0]
@@ -425,7 +493,7 @@
     )
     hg_ref[...] = dot_nt(eye, tot, HIGHEST)[0:3, 0:HEADS]
     stage("b", 5)
-    second_matmul(2)
+    second_matmul((2,), 0, FAR)
     for copy in pending:
         copy.wait_send()
 
@@ -440,7 +508,6 @@
 
 
 def body(upstream, out_weight, inner, groups_bc, dt_raw, a_log, skip, dt_bias, head_counts):
-    smem = pl.BlockSpec(memory_space=pltpu.SMEM)
     vmem = pl.BlockSpec(memory_space=pltpu.VMEM)
     hbm = pl.BlockSpec(memory_space=pl.ANY)
     dma = lambda n: pltpu.SemaphoreType.DMA((n,))
@@ -454,12 +521,17 @@
     results = pl.pallas_call(
         kernel,
         out_shape=tuple(pltpu.VMEM(*one) for one in shapes),
-        in_specs=[smem] * 4 + [vmem] + [hbm] * 4,
+        in_specs=[hbm] * 9,
         out_specs=(vmem,) * 5,
         scratch_shapes=[
+            pltpu.SMEM((HEADS,), F32),
+            pltpu.SMEM((HEADS,), F32),
+            pltpu.SMEM((HEADS,), F32),
+            pltpu.SMEM((NT,), jnp.int32),
+            pltpu.VMEM((HEADS, T), F32),
             pltpu.VMEM((NT, 16, D), BF16),
-            pltpu.VMEM((NT, DROWS, T), BF16),
-            pltpu.VMEM((NDP, 16, DROWS), BF16),
+            pltpu.VMEM((NT, KB, DROWS), BF16),
+            pltpu.VMEM((3, NT, 16, DROWS), BF16),
             pltpu.VMEM((NDP, T, WIDTH), BF16),
             pltpu.VMEM((D, WIDTH), BF16),
             pltpu.VMEM((T, WIDTH), BF16),
@@ -477,7 +549,7 @@
             pltpu.VMEM((T, WIDTH), F32),
             pltpu.VMEM((NDP, 16, HALF), F32),
             dma(2 * NK), dma(2 * NK), dma(2 * NK), dma(2 * NK),
-            dma(NDP), dma(NDP), dma(16), dma(16), dma(20), dma(20), dma(NDP), dma(NDP), dma(5),
+            dma(FAR), dma(FAR), dma(6), dma(6), dma(16), dma(16), dma(20), dma(20), dma(NDP), dma(NDP), dma(9),
         ],
         compiler_params=pltpu.CompilerParams(
             collective_id=0, has_side_effects=True, vmem_limit_bytes=56 * 1024 * 1024

time: 62.4 us -> 58.7 us (0.941)
  Pallas kernels: 61.6 us -> 57.9 us
    pallas_call x1, Pallas kernels: 60.3 us -> 56.6 us  [body(): pl.pallas_call(kernel, out_shape=tuple((pltpu.VMEM(*one) for one in shape...]
where the time goes in v3:
time: 58.7 us
  Pallas kernels  57.9 us (99%)
  between operations  0.8 us (1%)
    pallas_call x1, Pallas kernels, body(): pl.pallas_call(kernel, out_shape=tuple((pltpu.VMEM(*one) for one in shape...  56.6 us
    pallas_call x1, Pallas kernels, body(): pl.pallas_call(publish, out_shape=tuple((jax.ShapeDtypeStruct(*one) for o...  1.3 us

profile of v3, /device:TPU:1, one launch (start us, length us, event | category | flops | bytes accessed | tf_op | source)
XLA Modules:
  0.0 58.7 jit_solution(11454251596086927860)
XLA Ops:
  0.6 56.6 %shard_map.128 = (bf16[256,640]{1,0:T(8,128)(2,1)S(1)}, bf16[256,512]{1,0:T(8,128)(2,1)S(1)}, f32[10,256]{1,0:T(8,128)S(1)}, f32[512,640]{1,0:T(8,128)S(1)}, f32[3,10]{1,0:T(4,128)S(1)}) custom-call(f32[10]{0:T(128)} %alog_hbm.1, f32[10]{0:T(128)} %skip_hbm.1, f32[10]{0:T(128)} %bias_hbm.1, s32[16]{0:T(128)} %counts_hbm.1, f32[10,256]{1,0:T(8,128)} %dtraw_hbm.1, ...), custom_call_target="tpu_custom_call" | custom-call | tf_op jit(solution)/shard_map/pallas_call | solution.py:521
  57.2 1.3 %shard_map.129 = (bf16[256,640]{1,0:T(8,128)(2,1)}, bf16[256,512]{1,0:T(8,128)(2,1)}, f32[10,256]{1,0:T(8,128)}, f32[512,640]{1,0:T(8,128)}, f32[3,10]{1,0:T(4,128)}) custom-call(bf16[256,640]{1,0:T(8,128)(2,1)S(1)} %get-tuple-element.10.refs_0_, bf16[256,512]{1,0:T(8,128)(2,1)S(1)} %get-tuple-element.11.refs_1_, f32[10,256]{1,0:T(8,128)S(1)} %get-tuple-element.12.refs_2_, ...), custom_call_target="tpu_custom_call" | custom-call | tf_op jit(solution)/shard_map/pallas_call | solution.py:558

commit v4 on v3

--- a/solution.py
+++ b/solution.py
@@ -256,16 +256,8 @@
             hbuf.at[i], hbuf.at[there if incoming else i], h_send.at[r], h_recv.at[r], ((i + r) % NDP, j)
         )
 
-    up_copy.wait()
-    pl.semaphore_wait(barrier, len(peers))
-    stage("a", 0)
-    for n in range(FAR):
-        copy = swap(n, False)
-        copy.start()
-        pending.append(copy)
     for copy in small:
         copy.wait()
-
     row16 = lax.broadcasted_iota(jnp.int32, (16, T), 0)
 
     def fill(ref):
@@ -294,6 +286,18 @@
     pack[16:32, :] = dt
     cols[...] = jnp.transpose(pack[...])
 
+    up_copy.wait()
+    pl.semaphore_wait(barrier, len(peers))
+    stage("a", 0)
+
+    def swap_send(*which):
+        for n in which:
+            copy = swap(n, False)
+            copy.start()
+            pending.append(copy)
+
+    swap_send(*range(0, FAR, 2))
+
     in_copy.wait()
     bc_copy.wait()
     score[...] = dot_nt(bc_buf[:, NSTATE:], bc_buf[:, :NSTATE])
@@ -313,41 +317,41 @@
         b = lax.broadcasted_iota(jnp.int32, (rows_n, cols_n), 1) + col_start
         return a >= b if lower else a <= b
 
-    def forward_pair(pair):
+    def forward_pair(pair, block):
         lanes = slice(pair * HALF, (pair + 1) * HALF)
         values = x_buf[:, lanes]
         lane_skip = per_lane(lambda h: skip_ref[h], pair)
         lane_active = per_lane(active, pair)
-        for block in range(2):
-            end = (block + 1) * HALF
-            here = slice(block * HALF, end)
-            sides = []
-            for h in (2 * pair, 2 * pair + 1):
-                gap = rows[0, h : h + 1, 0:end] - cols[here, h : h + 1]
-                gap = jnp.where(causal(HALF, end, block * HALF, 0, True), gap, -1e30)
-                weights = jnp.exp(gap) * (score[here, 0:end] * rows[1, h : h + 1, 0:end])
-                high, low = split(weights)
-                sides.append(dot(high, values[0:end]) + dot(low, values[0:end]))
-            scanned = jnp.where(left, sides[0], sides[1])
-            yscan[here, lanes] = scanned
-            out = (scanned + lane_skip * values[here].astype(F32)) * lane_active
-            outs[FAR, here, lanes] = out.astype(BF16)
-
-    forward_pair(0)
-    forward_pair(1)
+        end = (block + 1) * HALF
+        here = slice(block * HALF, end)
+        sides = []
+        for h in (2 * pair, 2 * pair + 1):
+            gap = rows[0, h : h + 1, 0:end] - cols[here, h : h + 1]
+            gap = jnp.where(causal(HALF, end, block * HALF, 0, True), gap, -1e30)
+            weights = jnp.exp(gap) * (score[here, 0:end] * rows[1, h : h + 1, 0:end])
+            high, low = split(weights)
+            sides.append(dot(high, values[0:end]) + dot(low, values[0:end]))
+        scanned = jnp.where(left, sides[0], sides[1])
+        yscan[here, lanes] = scanned
+        out = (scanned + lane_skip * values[here].astype(F32)) * lane_active
+        outs[FAR, here, lanes] = out.astype(BF16)
+
+    for pair in range(5):
+        forward_pair(pair, 0)
+    ring_stage(0, 0)
+    forward_pair(0, 1)
     stage("a", 1)
-    forward_pair(2)
-    forward_pair(3)
-    forward_pair(4)
-    ring_stage(0, 0)
+    for pair in range(1, 5):
+        forward_pair(pair, 1)
     ring_stage(0, 1)
+    swap_send(*range(1, FAR, 2))
     stage("a", 2)
-    for n in range(FAR):
-        swap(n, True).wait_recv()
     ring_stage(1, 0)
     stage("a", 3)
     ring_stage(1, 1)
     stage("a", 4)
+    for n in range(FAR):
+        swap(n, True).wait_recv()
     stage("b", 0)
     ring_stage(2, 0)
     w_copy.wait()
@@ -356,7 +360,7 @@
     near_send(1, 0)
     ring_stage(2, 1)
 
-    depth = 1024
+    depth = 4096
 
     def first_matmul(step, carry):
         at = pl.multiple_of(step * depth, depth)
@@ -437,7 +441,6 @@
         pending.append(copy)
     near_send(1, 1, 2)
 
-    stage("b", 3)
     low_high, low_low = split(dgt[...])
     gg_ref[:, :NSTATE] = (dot(low_high, bc_buf[:, NSTATE:]) + dot(low_low, bc_buf[:, NSTATE:])).astype(BF16)
     up_high, up_low = split(jnp.transpose(dgt[...]))
@@ -471,8 +474,10 @@
             wg_ref[here, :] += dot_tn(left_side, outs[FAR + 2 :, :, :].reshape(2 * T, WIDTH))
 
     near_wait(0)
-    cross_waits((0, 1, 2, 3))
+    cross_waits((0, 1))
     chip_matmul()
+    stage("b", 3)
+    cross_waits((2, 3))
     second_matmul((0,), 0, MOST)
     stage("b", 4)
     ring_stage(4, 0)
@@ -492,9 +497,12 @@
         lax.broadcasted_iota(jnp.int32, (8, HALF), 0) == lax.broadcasted_iota(jnp.int32, (8, HALF), 1), 1.0, 0.0
     )
     hg_ref[...] = dot_nt(eye, tot, HIGHEST)[0:3, 0:HEADS]
+    last = 20
+    for copy in pending[:-last]:
+        copy.wait_send()
     stage("b", 5)
     second_matmul((2,), 0, FAR)
-    for copy in pending:
+    for copy in pending[-last:]:
         copy.wait_send()
 
 

time: 58.7 us -> 58 us (0.988)
  Pallas kernels: 57.9 us -> 57.2 us
    pallas_call x1, Pallas kernels: 56.6 us -> 55.9 us  [body(): pl.pallas_call(kernel, out_shape=tuple((pltpu.VMEM(*one) for one in shape...]
where the time goes in v4:
time: 58 us; the launch traced here: 57.9 us
  Pallas kernels  57.2 us (99%)
  between operations  0.64 us (1%)
    pallas_call x1, Pallas kernels, body(): pl.pallas_call(kernel, out_shape=tuple((pltpu.VMEM(*one) for one in shape...  55.9 us
    pallas_call x1, Pallas kernels, body(): pl.pallas_call(publish, out_shape=tuple((jax.ShapeDtypeStruct(*one) for o...  1.3 us

profile of v4, /device:TPU:1, one launch (start us, length us, event | category | flops | bytes accessed | tf_op | source)
XLA Modules:
  0.0 57.9 jit_solution(3116605092849124032)
XLA Ops:
  0.6 55.9 %shard_map.128 = (bf16[256,640]{1,0:T(8,128)(2,1)S(1)}, bf16[256,512]{1,0:T(8,128)(2,1)S(1)}, f32[10,256]{1,0:T(8,128)S(1)}, f32[512,640]{1,0:T(8,128)S(1)}, f32[3,10]{1,0:T(4,128)S(1)}) custom-call(f32[10]{0:T(128)} %alog_hbm.1, f32[10]{0:T(128)} %skip_hbm.1, f32[10]{0:T(128)} %bias_hbm.1, s32[16]{0:T(128)} %counts_hbm.1, f32[10,256]{1,0:T(8,128)} %dtraw_hbm.1, ...), custom_call_target="tpu_custom_call" | custom-call | tf_op jit(solution)/shard_map/pallas_call | solution.py:529
  56.6 1.3 %shard_map.129 = (bf16[256,640]{1,0:T(8,128)(2,1)}, bf16[256,512]{1,0:T(8,128)(2,1)}, f32[10,256]{1,0:T(8,128)}, f32[512,640]{1,0:T(8,128)}, f32[3,10]{1,0:T(4,128)}) custom-call(bf16[256,640]{1,0:T(8,128)(2,1)S(1)} %get-tuple-element.10.refs_0_, bf16[256,512]{1,0:T(8,128)(2,1)S(1)} %get-tuple-element.11.refs_1_, f32[10,256]{1,0:T(8,128)S(1)} %get-tuple-element.12.refs_2_, ...), custom_call_target="tpu_custom_call" | custom-call | tf_op jit(solution)/shard_map/pallas_call | solution.py:566

commit v5 on v4

--- a/solution.py
+++ b/solution.py
@@ -245,9 +245,9 @@
             copy.start()
             pending.append(copy)
 
-    def near_wait(*which):
+    def near_wait(halves, *which):
         for n in which:
-            for half in range(2):
+            for half in halves:
                 near_swap(n, half, True).wait_recv()
 
     def heads_swap(r, incoming):
@@ -467,13 +467,12 @@
             left_side = jnp.concatenate([mine, near[0, :, :, here].reshape(T, T)], axis=0)
             wg_ref[here, :] = dot_tn(left_side, outs[FAR : FAR + 2, :, :].reshape(2 * T, WIDTH))
 
-    def near_matmul():
-        for p in range(2):
-            here = slice(p * T, (p + 1) * T)
-            left_side = near[1:3, :, :, here].reshape(2 * T, T)
-            wg_ref[here, :] += dot_tn(left_side, outs[FAR + 2 :, :, :].reshape(2 * T, WIDTH))
-
-    near_wait(0)
+    def near_matmul(p):
+        here = slice(p * T, (p + 1) * T)
+        left_side = near[1:3, :, :, here].reshape(2 * T, T)
+        wg_ref[here, :] += dot_tn(left_side, outs[FAR + 2 :, :, :].reshape(2 * T, WIDTH))
+
+    near_wait((0, 1), 0)
     cross_waits((0, 1))
     chip_matmul()
     stage("b", 3)
@@ -482,12 +481,14 @@
     stage("b", 4)
     ring_stage(4, 0)
     ring_stage(4, 1)
+    near_wait((0,), 1, 2)
+    near_matmul(0)
     second_matmul((1,), 0, MOST)
     second_matmul((-1,), 0, MOST)
     cross_waits((4,))
     second_matmul((0, 1, -1), MOST, FAR)
-    near_wait(1, 2)
-    near_matmul()
+    near_wait((1,), 1, 2)
+    near_matmul(1)
     for r in range(1, NDP):
         heads_swap(r, True).wait_recv()
     tot = hbuf[0]

time: 58 us -> 57.8 us (level)
  no operation moved by 1% of the time
where the time goes in v5:
time: 57.8 us; the launch traced here: 57.7 us
  Pallas kernels  57.1 us (99%)
  between operations  0.64 us (1%)
    pallas_call x1, Pallas kernels, body(): pl.pallas_call(kernel, out_shape=tuple((pltpu.VMEM(*one) for one in shape...  55.8 us
    pallas_call x1, Pallas kernels, body(): pl.pallas_call(publish, out_shape=tuple((jax.ShapeDtypeStruct(*one) for o...  1.3 us

profile of v5, /device:TPU:1, one launch (start us, length us, event | category | flops | bytes accessed | tf_op | source)
XLA Modules:
  0.0 57.7 jit_solution(12424558378465424959)
XLA Ops:
  0.6 55.8 %shard_map.128 = (bf16[256,640]{1,0:T(8,128)(2,1)S(1)}, bf16[256,512]{1,0:T(8,128)(2,1)S(1)}, f32[10,256]{1,0:T(8,128)S(1)}, f32[512,640]{1,0:T(8,128)S(1)}, f32[3,10]{1,0:T(4,128)S(1)}) custom-call(f32[10]{0:T(128)} %alog_hbm.1, f32[10]{0:T(128)} %skip_hbm.1, f32[10]{0:T(128)} %bias_hbm.1, s32[16]{0:T(128)} %counts_hbm.1, f32[10,256]{1,0:T(8,128)} %dtraw_hbm.1, ...), custom_call_target="tpu_custom_call" | custom-call | tf_op jit(solution)/shard_map/pallas_call | solution.py:530
  56.4 1.3 %shard_map.129 = (bf16[256,640]{1,0:T(8,128)(2,1)}, bf16[256,512]{1,0:T(8,128)(2,1)}, f32[10,256]{1,0:T(8,128)}, f32[512,640]{1,0:T(8,128)}, f32[3,10]{1,0:T(4,128)}) custom-call(bf16[256,640]{1,0:T(8,128)(2,1)S(1)} %get-tuple-element.10.refs_0_, bf16[256,512]{1,0:T(8,128)(2,1)S(1)} %get-tuple-element.11.refs_1_, f32[10,256]{1,0:T(8,128)S(1)} %get-tuple-element.12.refs_2_, ...), custom_call_target="tpu_custom_call" | custom-call | tf_op jit(solution)/shard_map/pallas_call | solution.py:567
